TPU v7x, 512 devices: a whole 4x8x8 slice. The times are simulated.
512 devices in a mesh: scene: 4 (over x), dir: 2 (over z_hi), tile: 64 (over z_lo, y, core).
Axes of the slice: x: 4, y: 8, z: 8 (z_hi: 2, z_lo: 4; z = z_hi * 4 + z_lo), core: 2. Of those that a mesh axis runs over, the one named last changes fastest.
Arguments:
- tiles: bfloat16 [256, 16, 16, 384], P(('scene', 'tile')), parts along dimension 0, may hold values from -6 to 6
- cotangent: bfloat16 [256, 16, 16, 384], P(('scene', 'tile')), parts along dimension 0, may hold values from -6 to 6
- xproj_w: bfloat16 [2, 2, 384, 44], P('dir'), may hold values from -0.3125 to 0.3125
- dtproj_w: bfloat16 [2, 2, 12, 384], P('dir'), may hold values from -1.75 to 1.75
- dt_bias: float32 [2, 2, 384], P('dir'), may hold values from -6 to -4
- a_log: float32 [2, 2, 16, 384], P('dir'), as said below
- skip_d: float32 [2, 2, 384], P('dir'), may hold values from 0.5 to 1.5
Outputs:
- y_out: bfloat16 [256, 16, 16, 384], P(('scene', 'tile')), parts along dimension 0
- du_out: bfloat16 [256, 16, 16, 384], P(('scene', 'tile')), parts along dimension 0
- d_xproj: float32 [8, 2, 384, 44], P(('scene', 'dir')), parts along dimension 0
There are 4 independent parts, one for each index of `scene`. A program takes and returns all parts, laid end to end along the dimension named above; an argument that names none is the same for every part. Nothing has to cross between parts.
Inputs may be any that keep to these rules, and one draw needn't show every extreme that they name: `a_log`: every entry lies between log(0.5 / 16384) and log(15).
All inputs are finite; a program needn't handle non-finite values.
Results may differ from a plain program's by a relative error of at most 0.0025.
Values may be sent and summed in bfloat16 or wider, within the bound.
A program may use at most 128 MiB of HBM per device.

v0:
```python
import jax
import jax.numpy as jnp
from jax import lax
from jax.experimental import pallas as pl
from jax.experimental.pallas import tpu as pltpu
from jax.sharding import PartitionSpec as P

MESH = pl.DeviceIdType.MESH

E = 384
NS = 16
TS = 16
TOK = 256
LOG2E = 1.4426950408889634
LN2 = 0.6931471805599453
NT = (((1,), (1,)), ((), ()))
TN = (((0,), (0,)), ((), ()))
NN = (((1,), (0,)), ((), ()))


def dot(lhs, rhs, dims=NN):
    return lax.dot_general(lhs, rhs, dims, preferred_element_type=jnp.float32)


def halves(vals):
    top = vals.astype(jnp.bfloat16)
    return top, (vals - top.astype(jnp.float32)).astype(jnp.bfloat16)


def thirds(vals):
    top = vals.astype(jnp.bfloat16)
    rest = vals - top.astype(jnp.float32)
    return (top,) + halves(rest)


def swap_matrix():
    row = lax.broadcasted_iota(jnp.int32, (TOK, TOK), 0)
    col = lax.broadcasted_iota(jnp.int32, (TOK, TOK), 1)
    return ((row % TS) * TS + row // TS == col).astype(jnp.bfloat16)


def rounded(vals):
    return vals.astype(jnp.bfloat16).astype(jnp.float32)


def lane_block(et):
    return slice(et * 128, (et + 1) * 128)


def prepare(axis, io, sc):
    if axis == 0:
        swap = swap_matrix()
        xs = dot(swap, io.x[...])
        cs = dot(swap, io.cot[...])
        xb = xs.astype(jnp.bfloat16)
        sc.xb[...] = xb
    else:
        xb = io.x[...]
        xs = xb.astype(jnp.float32)
        cs = io.cot[...].astype(jnp.float32)
    sc.u[axis] = xs
    sc.cot[axis] = cs
    mixed = dot(xb, io.xw[axis])
    for n in range(2 * NS):
        sc.bc[axis, :, lane_block(n)] = jnp.broadcast_to(mixed[:, 12 + n : 13 + n], (TOK, 128))
    proj = io.dw[axis]
    raw = sum(dot(part, proj) for part in thirds(mixed))
    raw = raw + io.bias[axis : axis + 1, :]
    dt = jnp.maximum(raw, 0.0) + jnp.log1p(jnp.exp(-jnp.abs(raw)))
    sc.dt[axis] = dt
    sc.w[axis] = dt * xs
    sc.rate[axis] = -LOG2E * jnp.exp(io.alog[axis])
    size = dt[0:TS]
    for p in range(1, TS):
        size = size + dt[p * TS : (p + 1) * TS]
    sc.size[...] = size


def local_maps(axis, turn, sc):
    def unit(lh, carry):
        line0 = pl.multiple_of(lh * 8, 8)
        for et in range(3):
            lanes = lane_block(et)
            for half in range(2):
                ns = range(half * 8, half * 8 + 8)
                rates = [jnp.broadcast_to(sc.rate[axis, n : n + 1, lanes], (8, 128)) for n in ns]

                def step(t, state):
                    hs, qs, gs = state
                    rows = pl.ds(pl.multiple_of(turn(t, 15) * TS + line0, 8), 8)
                    dt = sc.dt[axis, rows, lanes]
                    w = sc.w[axis, rows, lanes]
                    ct = sc.cot[axis, rows, lanes]
                    nh, nq, ng = [], [], []
                    for m, n in enumerate(ns):
                        a = jnp.exp2(dt * rates[m])
                        nh.append(a * hs[m] + w * sc.bc[axis, rows, lane_block(n)])
                        q = a * qs[m]
                        nq.append(q)
                        ng.append(gs[m] + q * (sc.bc[axis, rows, lane_block(NS + n)] * ct))
                    return nh, nq, ng

                zero = [jnp.zeros((8, 128), jnp.float32)] * 8
                one = [jnp.ones((8, 128), jnp.float32)] * 8
                hs, qs, gs = lax.fori_loop(0, TS, step, (zero, one, zero))
                for m, n in enumerate(ns):
                    rows = pl.ds(pl.multiple_of(n * TS + line0, 8), 8)
                    sc.vals[0, et, rows, :] = hs[m]
                    sc.vals[1, et, rows, :] = gs[m]
        return carry

    lax.fori_loop(0, 2, unit, 0)

    def feed(k, state):
        out = []
        for sense in range(2):
            line = turn(k if sense == 0 else 15 - k, 15)
            size = 8.0 * sc.size[pl.ds(line, 1), :]
            for et in range(3):
                at = pl.ds(line, NS, stride=TS)
                decay = jnp.exp2(size[:, lane_block(et)] * sc.rate[axis, :, lane_block(et)])
                val = sc.vals[sense, et, at, :] + state[sense * 3 + et] * decay
                sent = rounded(val)
                sc.vals[sense, et, at, :] = sent
                out.append(val - sent)
        return out

    lax.fori_loop(0, TS, feed, [jnp.zeros((NS, 128), jnp.float32)] * 6)
    size = sc.size[...].astype(jnp.bfloat16)
    for j in range(8):
        for k in range(4):
            n = 2 * j + k % 2
            for et in range(3):
                sc.msg[axis, j, k, :, lane_block(et)] = sc.vals[k // 2, et, n * TS : (n + 1) * TS, :].astype(jnp.bfloat16)
        sc.msg[axis, j, 4] = size


def fold_lines(axis, pos, turn, sc):
    total = sc.recv[axis, 0, 4].astype(jnp.float32)
    for et in range(3):
        sc.before[axis, et, 0:TS, :] = jnp.zeros((TS, 128), jnp.float32)
    for tau in range(1, 8):
        for et in range(3):
            sc.before[axis, et, tau * TS : (tau + 1) * TS, :] = total[:, lane_block(et)]
        total = total + sc.recv[axis, tau, 4].astype(jnp.float32)
    sc.total[axis] = total
    for i in range(2):
        rate = sc.rate[axis, pl.ds(2 * pos + i, 1), :]

        def along(tau, state):
            d = jnp.exp2(sc.recv[axis, tau, 4].astype(jnp.float32) * rate)
            sc.decay[axis, i, tau] = d
            return d * state + sc.recv[axis, tau, i].astype(jnp.float32)

        sc.line[axis, i] = lax.fori_loop(0, 8, along, jnp.zeros((TS, E), jnp.float32))

        def against(k, state):
            tau = 7 - k
            return sc.decay[axis, i, tau] * state + sc.recv[axis, tau, 2 + i].astype(jnp.float32)

        sc.line[axis, 2 + i] = lax.fori_loop(0, 8, against, jnp.zeros((TS, E), jnp.float32))
        sc.line[axis, 4 + i] = jnp.exp2(total * rate)

    def fold(k, state):
        h0, h1, g0, g1 = state
        fw = pl.ds(turn(k, 15), 1)
        bw = pl.ds(turn(15 - k, 15), 1)
        return (sc.line[axis, 4, fw, :] * h0 + sc.line[axis, 0, fw, :], sc.line[axis, 5, fw, :] * h1 + sc.line[axis, 1, fw, :],
                sc.line[axis, 4, bw, :] * g0 + sc.line[axis, 2, bw, :], sc.line[axis, 5, bw, :] * g1 + sc.line[axis, 3, bw, :])

    ends = lax.fori_loop(0, TS, fold, (jnp.zeros((1, E), jnp.float32),) * 4)
    for i in range(4):
        sc.band_send[axis, i : i + 1, :] = ends[i]
    sc.band_send[axis, 4:5, :] = jnp.sum(total, axis=0, keepdims=True)
    sc.band_send[axis, 5:8, :] = jnp.zeros((3, E), jnp.float32)


def enter_lines(axis, pos, mine, turn, sc):
    zero = jnp.zeros((1, E), jnp.float32)
    rates = [sc.rate[axis, pl.ds(2 * pos + i, 1), :] for i in range(2)]
    starts = []
    for i in range(2):

        def ahead(tau, state):
            grown = jnp.exp2(sc.band_recv[axis, tau, 4:5, :] * rates[i]) * state + sc.band_recv[axis, tau, i : i + 1, :]
            return jnp.where(tau < mine, grown, state)

        def behind(k, state):
            tau = 7 - k
            grown = jnp.exp2(sc.band_recv[axis, tau, 4:5, :] * rates[i]) * state + sc.band_recv[axis, tau, 2 + i : 3 + i, :]
            return jnp.where(tau > mine, grown, state)

        starts.append((lax.fori_loop(0, 8, ahead, zero), lax.fori_loop(0, 8, behind, zero)))

    def advance(k, state):
        h0, h1, g0, g1 = state
        fw = pl.ds(turn(k, 15), 1)
        bw = pl.ds(turn(15 - k, 15), 1)
        new = (sc.line[axis, 4, fw, :] * h0 + sc.line[axis, 0, fw, :], sc.line[axis, 5, fw, :] * h1 + sc.line[axis, 1, fw, :],
               sc.line[axis, 4, bw, :] * g0 + sc.line[axis, 2, bw, :], sc.line[axis, 5, bw, :] * g1 + sc.line[axis, 3, bw, :])
        sc.line[axis, 0, fw, :] = h0
        sc.line[axis, 1, fw, :] = h1
        sc.line[axis, 2, bw, :] = g0
        sc.line[axis, 3, bw, :] = g1
        return new

    lax.fori_loop(0, TS, advance, (starts[0][0], starts[1][0], starts[0][1], starts[1][1]))

    def entry(tau, state):
        back = 7 - tau
        fw = pl.ds(pl.multiple_of(tau * TS, TS), TS)
        bw = pl.ds(pl.multiple_of(back * TS, TS), TS)
        for et in range(3):
            for i in range(2):
                sc.ent[i, et, fw, :] = state[i][:, lane_block(et)]
                sc.ent[2 + i, et, bw, :] = state[2 + i][:, lane_block(et)]
        return ([sc.decay[axis, i, tau] * state[i] + sc.recv[axis, tau, i].astype(jnp.float32) for i in range(2)]
                + [sc.decay[axis, i, back] * state[2 + i] + sc.recv[axis, back, 2 + i].astype(jnp.float32) for i in range(2)])

    lax.fori_loop(0, 8, entry, [sc.line[axis, k] for k in range(4)])

    def differ(k, state):
        out = []
        for et in range(3):
            lanes = lane_block(et)
            for sense in range(2):
                line = turn(k if sense == 0 else 15 - k, 15)
                at = pl.ds(line, 8, stride=TS)
                first = sc.before[axis, et, at, :]
                whole = sc.total[axis, pl.ds(line, 1), :][:, lanes]
                if sense == 1:
                    first = first + sc.own_f32[axis, et, at, :]
                    gap = state[6 * et + 3] + (whole - first)
                    left = first
                else:
                    gap = state[6 * et] + first
                    left = whole - first
                out.append(left)
                for i in range(2):
                    val = sc.ent[2 * sense + i, et, at, :]
                    guess = jnp.exp2(gap * rates[i][:, lanes]) * state[6 * et + 3 * sense + 1 + i]
                    sent = rounded(val - guess)
                    sc.ent[2 * sense + i, et, at, :] = sent
                    out.append(guess + sent)
        return out

    lax.fori_loop(0, TS, differ, [jnp.zeros((8, 128), jnp.float32)] * 18)
    for tau in range(8):
        for k in range(4):
            for et in range(3):
                sc.out[axis, tau, k, :, lane_block(et)] = sc.ent[k, et, tau * TS : (tau + 1) * TS, :].astype(jnp.bfloat16)


def decode(axis, slot, turn, sc):
    for j in range(8):
        for k in range(4):
            n = 2 * j + k % 2
            for et in range(3):
                sc.vals[k // 2, et, n * TS : (n + 1) * TS, :] = sc.back[axis, j, k, :, lane_block(et)].astype(jnp.float32)

    def add(k, state):
        out = []
        for et in range(3):
            lanes = lane_block(et)
            for sense in range(2):
                line = turn(k if sense == 0 else 15 - k, 15)
                own = pl.ds(slot * TS + line, 1)
                at = pl.ds(line, NS, stride=TS)
                first = sc.before[axis, et, own, :]
                whole = sc.total[axis, pl.ds(line, 1), :][:, lanes]
                if sense == 1:
                    first = first + sc.own_f32[axis, et, own, :]
                    gap = state[4 * et + 2] + (whole - first)
                    left = first
                else:
                    gap = state[4 * et] + first
                    left = whole - first
                val = jnp.exp2(gap * sc.rate[axis, :, lanes]) * state[4 * et + 2 * sense + 1] + sc.vals[sense, et, at, :]
                sc.vals[sense, et, at, :] = val
                out.append(left)
                out.append(val)
        return out

    lax.fori_loop(0, TS, add, [jnp.zeros((1, 128), jnp.float32), jnp.zeros((NS, 128), jnp.float32)] * 6)


def scan_tile(axis, turn, io, sc, sent_part):
    for et in range(3):
        lanes = lane_block(et)

        def unit(lh, carry):
            line0 = pl.multiple_of(lh * 8, 8)
            rates = [jnp.broadcast_to(sc.rate[axis, n : n + 1, lanes], (8, 128)) for n in range(NS)]
            skip = jnp.broadcast_to(io.skip[axis : axis + 1, lanes], (8, 128))

            def rows_at(t):
                return pl.ds(pl.multiple_of(turn(t, 15) * TS + line0, 8), 8)

            def start(sense):
                return [sc.vals[sense, et, pl.ds(pl.multiple_of(n * TS + line0, 8), 8), :] for n in range(NS)]

            def forward(t, hs):
                rows = rows_at(t)
                dt = sc.dt[axis, rows, lanes]
                w = sc.w[axis, rows, lanes]
                ct = sc.cot[axis, rows, lanes]
                y = skip * sc.u[axis, rows, lanes]
                out = []
                for n in range(NS):
                    a = jnp.exp2(dt * rates[n])
                    ah = a * hs[n]
                    sc.ah[t, n] = ah
                    h = ah + w * sc.bc[axis, rows, lane_block(n)]
                    cols = lane_block(NS + n)
                    y = y + h * sc.bc[axis, rows, cols]
                    dc = h * ct
                    if et > 0:
                        dc = dc + sc.dbc[rows, cols]
                    sc.dbc[rows, cols] = dc
                    out.append(h)
                if axis == 0:
                    sc.turned[0, et, rows, :] = y
                else:
                    sc.field[0, et, rows, :] = sc.field[0, et, rows, :] + y
                return out

            lax.fori_loop(0, TS, forward, start(0))

            def backward(i, gs):
                t = 15 - i
                rows = rows_at(t)
                dt = sc.dt[axis, rows, lanes]
                w = sc.w[axis, rows, lanes]
                ct = sc.cot[axis, rows, lanes]
                dw = jnp.zeros((8, 128), jnp.float32)
                dr = jnp.zeros((8, 128), jnp.float32)
                out = []
                for n in range(NS):
                    a = jnp.exp2(dt * rates[n])
                    g = gs[n] + sc.bc[axis, rows, lane_block(NS + n)] * ct
                    cols = lane_block(n)
                    db = g * w
                    if et > 0:
                        db = db + sc.dbc[rows, cols]
                    sc.dbc[rows, cols] = db
                    dw = dw + g * sc.bc[axis, rows, cols]
                    dr = dr + (g * sc.ah[t, n]) * rates[n]
                    out.append(a * g)
                sc.ddt[rows, lanes] = dr * LN2 + dw * sc.u[axis, rows, lanes]
                du = dw * dt + skip * ct
                if axis == 0:
                    sc.turned[1, et, rows, :] = du
                else:
                    sc.field[1, et, rows, :] = sc.field[1, et, rows, :] + du
                return out

            lax.fori_loop(0, TS, backward, start(1))
            return carry

        lax.fori_loop(0, 2, unit, 0)
        sent_part(et)


def project_back(axis, io, sc):
    dt = sc.dt[axis]
    small = dt * (1.0 - dt * (0.5 - dt * (1.0 / 6.0 - dt * (1.0 / 24.0))))
    dv = sc.ddt[...] * jnp.where(dt < 0.03, small, 1.0 - jnp.exp(-dt))
    proj = io.dw[axis]
    dmix = sum(dot(part, proj, NT) for part in halves(dv))
    row = lax.broadcasted_iota(jnp.int32, (512, 128), 0)
    col = lax.broadcasted_iota(jnp.int32, (512, 128), 1)
    for blk in range(8):
        pick = (col == 12 + blk * 4 + row // 128).astype(jnp.bfloat16)
        for part in halves(sc.dbc[:, blk * 512 : (blk + 1) * 512]):
            dmix = dmix + dot(part, pick)
    parts = halves(dmix)
    weight = io.xw[axis]
    xb = sc.xb[...] if axis == 0 else io.x[...]
    dx = sum(dot(part, xb, TN) for part in parts)
    for q in range(4):
        sc.dx_src[4 * axis + q] = dx[q * TS : (q + 1) * TS]
    return sum(dot(part, weight, NT) for part in parts)


class Refs:
    def __init__(self, names, refs):
        self.__dict__.update(zip(names, refs))


INPUTS = ("x", "cot", "xw", "dw", "bias", "alog", "skip")


def layer_kernel(*refs):
    hbm = refs[:7]
    yo_ref, duo_ref, dxo_ref = refs[7:10]
    sc = Refs(SCRATCH, refs[10:])
    io = Refs(INPUTS, [getattr(sc, "in_" + name) for name in INPUTS])
    tile = lax.axis_index("tile")
    side = lax.axis_index("dir")
    other = 1 - side
    row, col = tile // 8, tile % 8
    along_row = [row * 8 + lax.rem(col + d, 8) for d in range(1, 8)]
    along_col = [lax.rem(row + d, 8) * 8 + col for d in range(1, 8)]
    peers = (along_row, along_col)
    place = ((col, row), (row, col))
    partner = {"dir": other}

    def turn(i, last):
        return side * last + (1 - 2 * side) * i

    barrier = pltpu.get_barrier_semaphore()
    for peer in along_row + along_col:
        pl.semaphore_signal(barrier, inc=1, device_id={"tile": peer}, device_id_type=MESH)
    pl.semaphore_signal(barrier, inc=1, device_id=partner, device_id_type=MESH)
    loads = [pltpu.make_async_copy(hbm[k], getattr(sc, "in_" + name), sc.sem_in.at[k]) for k, name in enumerate(INPUTS)]
    for load in loads:
        load.start()
    for load in loads:
        load.wait()

    def push(src, dst, sems, slot, where):
        copy = pltpu.make_async_remote_copy(
            src_ref=src, dst_ref=dst, send_sem=sems.at[(0,) + slot], recv_sem=sems.at[(1,) + slot],
            device_id=where, device_id_type=MESH)
        copy.start()
        return copy

    there, bands, backs = [], [], []
    for axis in range(2):
        prepare(axis, io, sc)
        local_maps(axis, turn, sc)
        if axis == 0:
            pl.semaphore_wait(barrier, 15)
        pos = place[axis][0]
        slot = turn(pos, 7)
        there.append([
            push(sc.msg.at[axis, lax.rem(pos + d, 8)], sc.recv.at[axis, slot], sc.sem_there, (axis, d - 1), {"tile": peers[axis][d - 1]})
            for d in range(1, 8)])
        sc.recv[axis, slot] = sc.msg[axis, pos]
    for axis in range(2):
        pos, band = place[axis]
        for copy in there[axis]:
            copy.wait_recv()
        for tau in range(8):
            for et in range(3):
                sc.own_f32[axis, et, tau * TS : (tau + 1) * TS, :] = sc.recv[axis, tau, 4, :, lane_block(et)].astype(jnp.float32)
        fold_lines(axis, pos, turn, sc)
        slot = turn(band, 7)
        bands.append([
            push(sc.band_send.at[axis], sc.band_recv.at[axis, slot], sc.sem_band, (axis, d - 1), {"tile": peers[1 - axis][d - 1]})
            for d in range(1, 8)])
        sc.band_recv[axis, slot] = sc.band_send[axis]
    for axis in range(2):
        pos, band = place[axis]
        for copy in bands[axis]:
            copy.wait_recv()
        enter_lines(axis, pos, turn(band, 7), turn, sc)
        backs.append([
            push(sc.out.at[axis, turn(lax.rem(pos + d, 8), 7)], sc.back.at[axis, pos], sc.sem_back, (axis, d - 1), {"tile": peers[axis][d - 1]})
            for d in range(1, 8)])
        sc.back[axis, pos] = sc.out[axis, turn(pos, 7)]

    halves_sent = [[], []]
    other_rows = pl.ds(pl.multiple_of(other * 128, 128), 128)
    own_rows = pl.ds(pl.multiple_of(side * 128, 128), 128)

    def send_half(kind, et):
        halves_sent[kind].append(push(sc.field.at[kind, et, other_rows, :], sc.half.at[kind, et], sc.sem_half, (kind, et), partner))

    for axis in range(2):
        for copy in backs[axis]:
            copy.wait_recv()
        decode(axis, turn(place[axis][0], 7), turn, sc)
        scan_tile(axis, turn, io, sc, (lambda et: None) if axis == 0 else (lambda et: send_half(0, et)))
        through = project_back(axis, io, sc)
        for et in range(3):
            if axis == 0:
                sc.turned[1, et] = sc.turned[1, et] + through[:, lane_block(et)]
                for kind in range(2):
                    for i in range(TS):
                        sc.field[kind, et, i * TS : (i + 1) * TS, :] = sc.turned[kind, et, pl.ds(i, TS, stride=TS), :]
            else:
                sc.field[1, et] = sc.field[1, et] + through[:, lane_block(et)]
                send_half(1, et)
    first = [push(sc.dx_src.at[lax.rem(col + d, 8)], sc.dx_one.at[col], sc.sem_dx, (0, d - 1), {"tile": along_row[d - 1]}) for d in range(1, 8)]
    sc.dx_one[col] = sc.dx_src[col]
    outs = []

    def merge(kind):
        for et in range(3):
            halves_sent[kind][et].wait_recv()
            sc.res[kind, own_rows, lane_block(et)] = (sc.field[kind, et, own_rows, :] + sc.half[kind, et]).astype(jnp.bfloat16)
        outs.append(push(sc.res.at[kind, own_rows, :], sc.res.at[kind, own_rows, :], sc.sem_out, (kind,), partner))

    merge(0)
    for copy in first:
        copy.wait_recv()
    sc.dx_two[row] = sum(sc.dx_one[j] for j in range(8))
    second = [push(sc.dx_two.at[row], sc.dx_two.at[row], sc.sem_dx, (1, d - 1), {"tile": along_col[d - 1]}) for d in range(1, 8)]
    merge(1)
    for copy in second:
        copy.wait_recv()
    sc.dx_all[col] = sum(sc.dx_two[j] for j in range(8))
    third = [push(sc.dx_all.at[col], sc.dx_all.at[col], sc.sem_dx, (2, d - 1), {"tile": along_row[d - 1]}) for d in range(1, 8)]
    outs[0].wait_recv()
    yo_ref[...] = sc.res[0]
    for copy in third:
        copy.wait_recv()
    dxo_ref[...] = sc.dx_all[...]
    outs[1].wait_recv()
    duo_ref[...] = sc.res[1]
    for group in there + bands + backs + halves_sent + [outs, first, second, third]:
        for copy in group:
            copy.wait_send()


def f32_buf(*shape):
    return pltpu.VMEM(shape, jnp.float32)


def bf16_buf(*shape):
    return pltpu.VMEM(shape, jnp.bfloat16)


def dma_sems(*shape):
    return pltpu.SemaphoreType.DMA(shape)


BUFFERS = {
    "in_x": bf16_buf(TOK, E), "in_cot": bf16_buf(TOK, E), "in_xw": bf16_buf(2, E, 128), "in_dw": bf16_buf(2, 128, E),
    "in_bias": f32_buf(2, E), "in_alog": f32_buf(2, NS, E), "in_skip": f32_buf(2, E), "sem_in": dma_sems(7),
    "xb": bf16_buf(TOK, E),
    "u": f32_buf(2, TOK, E), "cot": f32_buf(2, TOK, E), "dt": f32_buf(2, TOK, E), "w": f32_buf(2, TOK, E),
    "bc": f32_buf(2, TOK, 4096), "rate": f32_buf(2, NS, E), "size": f32_buf(TS, E),
    "vals": f32_buf(2, 3, NS * TS, 128),
    "msg": bf16_buf(2, 8, 5, TS, E), "recv": bf16_buf(2, 8, 5, TS, E),
    "before": f32_buf(2, 3, 8 * TS, 128), "own_f32": f32_buf(2, 3, 8 * TS, 128), "total": f32_buf(2, TS, E),
    "decay": f32_buf(2, 2, 8, TS, E), "line": f32_buf(2, 6, TS, E),
    "band_send": f32_buf(2, 8, E), "band_recv": f32_buf(2, 8, 8, E),
    "ent": f32_buf(4, 3, 8 * TS, 128),
    "out": bf16_buf(2, 8, 4, TS, E), "back": bf16_buf(2, 8, 4, TS, E),
    "dbc": f32_buf(TOK, 4096), "ah": f32_buf(TS, NS, 8, 128), "ddt": f32_buf(TOK, E),
    "turned": f32_buf(2, 3, TOK, 128), "field": f32_buf(2, 3, TOK, 128),
    "half": f32_buf(2, 3, 128, 128), "res": bf16_buf(2, TOK, E),
    "dx_src": f32_buf(8, TS, E), "dx_one": f32_buf(8, TS, E), "dx_two": f32_buf(8, TS, E), "dx_all": f32_buf(8, TS, E),
    "sem_there": dma_sems(2, 2, 7), "sem_band": dma_sems(2, 2, 7), "sem_back": dma_sems(2, 2, 7),
    "sem_half": dma_sems(2, 2, 3), "sem_out": dma_sems(2, 2), "sem_dx": dma_sems(2, 3, 7),
}
SCRATCH = tuple(BUFFERS)
VMEM = pl.BlockSpec(memory_space=pltpu.VMEM)


def local(tiles, cotangent, xproj_w, dtproj_w, dt_bias, a_log, skip_d):
    xw = jnp.pad(xproj_w[0], ((0, 0), (0, 0), (0, 84)))
    dw = jnp.pad(dtproj_w[0], ((0, 0), (0, 116), (0, 0)))
    out = jax.ShapeDtypeStruct((TOK, E), jnp.bfloat16)
    yo, duo, dxo = pl.pallas_call(
        layer_kernel,
        out_shape=(out, out, jax.ShapeDtypeStruct((8, TS, E), jnp.float32)),
        in_specs=[pl.BlockSpec(memory_space=pl.ANY)] * 7,
        out_specs=(VMEM,) * 3,
        scratch_shapes=list(BUFFERS.values()),
        compiler_params=pltpu.CompilerParams(vmem_limit_bytes=56 * 2**20, collective_id=0, has_side_effects=True),
        name="layer",
    )(tiles.reshape(TOK, E), cotangent.reshape(TOK, E), xw, dw, dt_bias[0], a_log[0], skip_d[0])
    dxo = dxo.reshape(2, 64, E)[:, :44].transpose(0, 2, 1)
    return yo.reshape(tiles.shape), duo.reshape(tiles.shape), dxo[None]


def solution(mesh):
    by_tile = P(("scene", "tile"), None, None, None)
    by_dir = P("dir", None, None, None)
    return jax.shard_map(
        local,
        mesh=mesh,
        in_specs=(by_tile, by_tile, by_dir, by_dir, P("dir", None, None), by_dir, P("dir", None, None)),
        out_specs=(by_tile, by_tile, P(("scene", "dir"), None, None, None)),
        check_vma=False,
    )
```

profile of v0, /device:TPU:1, one launch (start us, length us, event | category | flops | bytes accessed | tf_op | source)
XLA Modules:
  0.0 120.2 jit_solution(6241225843614933961)
XLA Ops:
  0.6 0.7 copy.17
  1.4 0.0 copy-start.2
  1.4 0.7 pad.9.refs_3_
  2.1 0.2 copy-done.2
  2.2 0.2 copy.10
  2.4 0.7 pad.8.refs_2_
  3.2 113.5 %layer.1 = (bf16[256,384]{1,0:T(8,128)(2,1)}, bf16[256,384]{1,0:T(8,128)(2,1)}, f32[8,16,384]{2,1,0:T(8,128)}) custom-call(bf16[256,384]{1,0:T(8,128)(2,1)} %bitcast.20, bf16[256,384]{1,0:T(8,128)(2,1)} %bitcast.21, bf16[2,384,128]{2,1,0:T(8,128)(2,1)} %pad.8.refs_2_, bf16[2,128,384]{2,1,0:T(8,128)(2,1)} %pad.9.refs_3_, f32[2,384]{1,0:T(2,128)} %bitcast.26, ...), custom_call_target="tpu_custom_call" | custom-call | tf_op jit(solution)/shard_map/layer/pallas_call | solution.py:557
  116.7 0.9 slice.4
  117.6 0.0 copy-start.1
  117.6 0.7 copy.16
  118.4 0.2 copy-done.1
  118.6 0.0 copy-start
  118.6 0.7 copy.20
  119.2 0.3 copy-done
  119.6 0.7 copy.21
Async XLA Ops:
  1.4 0.9 copy-start.2
  117.6 0.9 copy-start.1
  118.6 1.0 copy-start
where the time goes:
time: 121 us; the launch traced here: 120 us
  Pallas kernels  114 us (94%)
  local copies, waits for them, and re-layouts  6.05 us (5%)
    pallas_call x1, Pallas kernels, local(): pl.pallas_call(layer_kernel, out_shape=(out, out, jax.ShapeDtypeStruct((8...  114 us
    unnamed x11, local copies, waits for them, and re-layouts  3.7 us

commit v1 on v0

v1 whole, which is shorter than its diff:
```python
import jax
import jax.numpy as jnp
from jax import lax
from jax.experimental import pallas as pl
from jax.experimental.pallas import tpu as pltpu
from jax.sharding import PartitionSpec as P

MESH = pl.DeviceIdType.MESH

E = 384
NS = 16
TS = 16
TOK = 256
LOG2E = 1.4426950408889634
LN2 = 0.6931471805599453
NT = (((1,), (1,)), ((), ()))
TN = (((0,), (0,)), ((), ()))
NN = (((1,), (0,)), ((), ()))


def dot(lhs, rhs, dims=NN):
    return lax.dot_general(lhs, rhs, dims, preferred_element_type=jnp.float32)


def halves(vals):
    top = vals.astype(jnp.bfloat16)
    return top, (vals - top.astype(jnp.float32)).astype(jnp.bfloat16)


def thirds(vals):
    top = vals.astype(jnp.bfloat16)
    rest = vals - top.astype(jnp.float32)
    return (top,) + halves(rest)


def swap_matrix():
    row = lax.broadcasted_iota(jnp.int32, (TOK, TOK), 0)
    col = lax.broadcasted_iota(jnp.int32, (TOK, TOK), 1)
    return ((row % TS) * TS + row // TS == col).astype(jnp.bfloat16)


def rounded(vals):
    return vals.astype(jnp.bfloat16).astype(jnp.float32)


def lane_block(et):
    return slice(et * 128, (et + 1) * 128)


def prepare(axis, io, sc):
    if axis == 0:
        swap = swap_matrix()
        xs = dot(swap, io.x[...])
        cs = dot(swap, io.cot[...])
        xb = xs.astype(jnp.bfloat16)
    else:
        xb = io.x[...]
        xs = xb.astype(jnp.float32)
        cs = io.cot[...].astype(jnp.float32)
    sc.u[axis] = xs.reshape(TS, TS, E)
    sc.cot[axis] = cs.reshape(TS, TS, E)
    for given, kept, count in ((io.xw, sc.xw, 44), (io.dw, sc.dw, 12)):
        sc.padded[...] = jnp.zeros((128, E), jnp.float32)
        sc.padded[0:count, :] = given[...].astype(jnp.float32)[:, axis, :]
        kept[axis] = sc.padded[...].astype(jnp.bfloat16)
    mixed = dot(xb, sc.xw[axis], NT)
    for n in range(2 * NS):
        sc.bc[axis, :, :, lane_block(n)] = jnp.broadcast_to(mixed[:, 12 + n : 13 + n], (TOK, 128)).reshape(TS, TS, 128)
    proj = sc.dw[axis]
    raw = sum(dot(part, proj) for part in thirds(mixed))
    raw = raw + io.bias[axis : axis + 1, :]
    dt = jnp.maximum(raw, 0.0) + jnp.log1p(jnp.exp(-jnp.abs(raw)))
    sc.dt[axis] = dt.reshape(TS, TS, E)
    sc.w[axis] = (dt * xs).reshape(TS, TS, E)
    sc.rate[axis] = -LOG2E * jnp.exp(io.alog[axis])
    size = dt[0:TS]
    for p in range(1, TS):
        size = size + dt[p * TS : (p + 1) * TS]
    sc.size[...] = size


def local_maps(axis, half, turn, sc):
    ns = range(half * 8, half * 8 + 8)

    def unit(lh, carry):
        line0 = pl.multiple_of(lh * 8, 8)
        lines = pl.ds(line0, 8)
        for et in range(3):
            lanes = lane_block(et)
            rates = [jnp.broadcast_to(sc.rate[axis, n : n + 1, lanes], (8, 128)) for n in ns]

            def step(t, state):
                hs, qs, gs = state
                p = turn(t, 15)
                dt = sc.dt[axis, p, lines, lanes]
                w = sc.w[axis, p, lines, lanes]
                ct = sc.cot[axis, p, lines, lanes]
                nh, nq, ng = [], [], []
                for m, n in enumerate(ns):
                    a = jnp.exp2(dt * rates[m])
                    nh.append(a * hs[m] + w * sc.bc[axis, p, lines, lane_block(n)])
                    q = a * qs[m]
                    nq.append(q)
                    ng.append(gs[m] + q * (sc.bc[axis, p, lines, lane_block(NS + n)] * ct))
                return nh, nq, ng

            zero = [jnp.zeros((8, 128), jnp.float32)] * 8
            one = [jnp.ones((8, 128), jnp.float32)] * 8
            hs, qs, gs = lax.fori_loop(0, TS, step, (zero, one, zero))
            for m, n in enumerate(ns):
                rows = pl.ds(pl.multiple_of(n * TS + line0, 8), 8)
                sc.vals[axis, 0, et, rows, :] = hs[m]
                sc.vals[axis, 1, et, rows, :] = gs[m]
        return carry

    lax.fori_loop(0, 2, unit, 0)

    def feed(k, state):
        out = []
        for sense in range(2):
            line = turn(k if sense == 0 else 15 - k, 15)
            size = 8.0 * sc.size[pl.ds(line, 1), :]
            for et in range(3):
                at = pl.ds(half * 8 * TS + line, 8, stride=TS)
                decay = jnp.exp2(size[:, lane_block(et)] * sc.rate[axis, half * 8 : half * 8 + 8, lane_block(et)])
                val = sc.vals[axis, sense, et, at, :] + state[sense * 3 + et] * decay
                sent = rounded(val)
                sc.vals[axis, sense, et, at, :] = sent
                out.append(val - sent)
        return out

    lax.fori_loop(0, TS, feed, [jnp.zeros((8, 128), jnp.float32)] * 6)
    size = sc.size[...].astype(jnp.bfloat16)
    for j in range(half * 4, half * 4 + 4):
        for k in range(4):
            n = 2 * j + k % 2
            for et in range(3):
                sc.msg[axis, j, k, :, lane_block(et)] = sc.vals[axis, k // 2, et, n * TS : (n + 1) * TS, :].astype(jnp.bfloat16)
        sc.msg[axis, j, 4] = size


def fold_lines(axis, pos, turn, sc):
    total = sc.recv[axis, 0, 4].astype(jnp.float32)
    for et in range(3):
        sc.before[axis, et, 0:TS, :] = jnp.zeros((TS, 128), jnp.float32)
    for tau in range(1, 8):
        for et in range(3):
            sc.before[axis, et, tau * TS : (tau + 1) * TS, :] = total[:, lane_block(et)]
        total = total + sc.recv[axis, tau, 4].astype(jnp.float32)
    sc.total[axis] = total
    for i in range(2):
        rate = sc.rate[axis, pl.ds(2 * pos + i, 1), :]

        def along(tau, state):
            d = jnp.exp2(sc.recv[axis, tau, 4].astype(jnp.float32) * rate)
            sc.decay[axis, i, tau] = d
            return d * state + sc.recv[axis, tau, i].astype(jnp.float32)

        sc.line[axis, i] = lax.fori_loop(0, 8, along, jnp.zeros((TS, E), jnp.float32))

        def against(k, state):
            tau = 7 - k
            return sc.decay[axis, i, tau] * state + sc.recv[axis, tau, 2 + i].astype(jnp.float32)

        sc.line[axis, 2 + i] = lax.fori_loop(0, 8, against, jnp.zeros((TS, E), jnp.float32))
        sc.line[axis, 4 + i] = jnp.exp2(total * rate)

    def fold(k, state):
        h0, h1, g0, g1 = state
        fw = pl.ds(turn(k, 15), 1)
        bw = pl.ds(turn(15 - k, 15), 1)
        return (sc.line[axis, 4, fw, :] * h0 + sc.line[axis, 0, fw, :], sc.line[axis, 5, fw, :] * h1 + sc.line[axis, 1, fw, :],
                sc.line[axis, 4, bw, :] * g0 + sc.line[axis, 2, bw, :], sc.line[axis, 5, bw, :] * g1 + sc.line[axis, 3, bw, :])

    ends = lax.fori_loop(0, TS, fold, (jnp.zeros((1, E), jnp.float32),) * 4)
    for i in range(4):
        sc.band_send[axis, i : i + 1, :] = ends[i]
    sc.band_send[axis, 4:5, :] = jnp.sum(total, axis=0, keepdims=True)
    sc.band_send[axis, 5:8, :] = jnp.zeros((3, E), jnp.float32)


def enter_lines(axis, pos, mine, turn, sc):
    zero = jnp.zeros((1, E), jnp.float32)
    rates = [sc.rate[axis, pl.ds(2 * pos + i, 1), :] for i in range(2)]
    starts = []
    for i in range(2):

        def ahead(tau, state):
            grown = jnp.exp2(sc.band_recv[axis, tau, 4:5, :] * rates[i]) * state + sc.band_recv[axis, tau, i : i + 1, :]
            return jnp.where(tau < mine, grown, state)

        def behind(k, state):
            tau = 7 - k
            grown = jnp.exp2(sc.band_recv[axis, tau, 4:5, :] * rates[i]) * state + sc.band_recv[axis, tau, 2 + i : 3 + i, :]
            return jnp.where(tau > mine, grown, state)

        starts.append((lax.fori_loop(0, 8, ahead, zero), lax.fori_loop(0, 8, behind, zero)))

    def advance(k, state):
        h0, h1, g0, g1 = state
        fw = pl.ds(turn(k, 15), 1)
        bw = pl.ds(turn(15 - k, 15), 1)
        new = (sc.line[axis, 4, fw, :] * h0 + sc.line[axis, 0, fw, :], sc.line[axis, 5, fw, :] * h1 + sc.line[axis, 1, fw, :],
               sc.line[axis, 4, bw, :] * g0 + sc.line[axis, 2, bw, :], sc.line[axis, 5, bw, :] * g1 + sc.line[axis, 3, bw, :])
        sc.line[axis, 0, fw, :] = h0
        sc.line[axis, 1, fw, :] = h1
        sc.line[axis, 2, bw, :] = g0
        sc.line[axis, 3, bw, :] = g1
        return new

    lax.fori_loop(0, TS, advance, (starts[0][0], starts[1][0], starts[0][1], starts[1][1]))

    def entry(tau, state):
        back = 7 - tau
        fw = pl.ds(pl.multiple_of(tau * TS, TS), TS)
        bw = pl.ds(pl.multiple_of(back * TS, TS), TS)
        for et in range(3):
            for i in range(2):
                sc.ent[i, et, fw, :] = state[i][:, lane_block(et)]
                sc.ent[2 + i, et, bw, :] = state[2 + i][:, lane_block(et)]
        return ([sc.decay[axis, i, tau] * state[i] + sc.recv[axis, tau, i].astype(jnp.float32) for i in range(2)]
                + [sc.decay[axis, i, back] * state[2 + i] + sc.recv[axis, back, 2 + i].astype(jnp.float32) for i in range(2)])

    lax.fori_loop(0, 8, entry, [sc.line[axis, k] for k in range(4)])

    def differ(k, state):
        out = []
        for et in range(3):
            lanes = lane_block(et)
            for sense in range(2):
                line = turn(k if sense == 0 else 15 - k, 15)
                at = pl.ds(line, 8, stride=TS)
                first = sc.before[axis, et, at, :]
                whole = sc.total[axis, pl.ds(line, 1), :][:, lanes]
                if sense == 1:
                    first = first + sc.own_f32[axis, et, at, :]
                    gap = state[6 * et + 3] + (whole - first)
                    left = first
                else:
                    gap = state[6 * et] + first
                    left = whole - first
                out.append(left)
                for i in range(2):
                    val = sc.ent[2 * sense + i, et, at, :]
                    guess = jnp.exp2(gap * rates[i][:, lanes]) * state[6 * et + 3 * sense + 1 + i]
                    sent = rounded(val - guess)
                    sc.ent[2 * sense + i, et, at, :] = sent
                    out.append(guess + sent)
        return out

    lax.fori_loop(0, TS, differ, [jnp.zeros((8, 128), jnp.float32)] * 18)
    for tau in range(8):
        for k in range(4):
            for et in range(3):
                sc.out[axis, tau, k, :, lane_block(et)] = sc.ent[k, et, tau * TS : (tau + 1) * TS, :].astype(jnp.bfloat16)


def decode(axis, slot, turn, sc):
    for j in range(8):
        for k in range(4):
            n = 2 * j + k % 2
            for et in range(3):
                sc.vals[axis, k // 2, et, n * TS : (n + 1) * TS, :] = sc.back[axis, j, k, :, lane_block(et)].astype(jnp.float32)

    def add(k, state):
        out = []
        for et in range(3):
            lanes = lane_block(et)
            for sense in range(2):
                line = turn(k if sense == 0 else 15 - k, 15)
                own = pl.ds(slot * TS + line, 1)
                at = pl.ds(line, NS, stride=TS)
                first = sc.before[axis, et, own, :]
                whole = sc.total[axis, pl.ds(line, 1), :][:, lanes]
                if sense == 1:
                    first = first + sc.own_f32[axis, et, own, :]
                    gap = state[4 * et + 2] + (whole - first)
                    left = first
                else:
                    gap = state[4 * et] + first
                    left = whole - first
                val = jnp.exp2(gap * sc.rate[axis, :, lanes]) * state[4 * et + 2 * sense + 1] + sc.vals[axis, sense, et, at, :]
                sc.vals[axis, sense, et, at, :] = val
                out.append(left)
                out.append(val)
        return out

    lax.fori_loop(0, TS, add, [jnp.zeros((1, 128), jnp.float32), jnp.zeros((NS, 128), jnp.float32)] * 6)


def scan_forward(axis, et, lh, turn, io, sc):
    line0 = pl.multiple_of(lh * 8, 8)
    lines = pl.ds(line0, 8)
    lanes = lane_block(et)
    rates = [jnp.broadcast_to(sc.rate[axis, n : n + 1, lanes], (8, 128)) for n in range(NS)]
    skip = jnp.broadcast_to(io.skip[axis : axis + 1, lanes], (8, 128))

    def forward(t, hs):
        p = turn(t, 15)
        dt = sc.dt[axis, p, lines, lanes]
        w = sc.w[axis, p, lines, lanes]
        ct = sc.cot[axis, p, lines, lanes]
        y = skip * sc.u[axis, p, lines, lanes]
        out = []
        for n in range(NS):
            a = jnp.exp2(dt * rates[n])
            ah = a * hs[n]
            sc.ah[axis, et, lh, t, n] = ah
            h = ah + w * sc.bc[axis, p, lines, lane_block(n)]
            cols = lane_block(NS + n)
            y = y + h * sc.bc[axis, p, lines, cols]
            dc = h * ct
            if et > 0:
                dc = dc + sc.dbc[axis, p, lines, cols]
            sc.dbc[axis, p, lines, cols] = dc
            out.append(h)
        if axis == 0:
            sc.turned[0, et, pl.ds(pl.multiple_of(p * TS + line0, 8), 8), :] = y
        else:
            sc.field[0, et, p, lines, :] = sc.field[0, et, p, lines, :] + y
        return out

    lax.fori_loop(0, TS, forward, [sc.vals[axis, 0, et, pl.ds(pl.multiple_of(n * TS + line0, 8), 8), :] for n in range(NS)])


def scan_backward(axis, et, lh, turn, io, sc):
    line0 = pl.multiple_of(lh * 8, 8)
    lines = pl.ds(line0, 8)
    lanes = lane_block(et)
    rates = [jnp.broadcast_to(sc.rate[axis, n : n + 1, lanes], (8, 128)) for n in range(NS)]
    skip = jnp.broadcast_to(io.skip[axis : axis + 1, lanes], (8, 128))

    def backward(i, gs):
        t = 15 - i
        p = turn(t, 15)
        dt = sc.dt[axis, p, lines, lanes]
        w = sc.w[axis, p, lines, lanes]
        ct = sc.cot[axis, p, lines, lanes]
        dw = jnp.zeros((8, 128), jnp.float32)
        dr = jnp.zeros((8, 128), jnp.float32)
        out = []
        for n in range(NS):
            a = jnp.exp2(dt * rates[n])
            g = gs[n] + sc.bc[axis, p, lines, lane_block(NS + n)] * ct
            cols = lane_block(n)
            db = g * w
            if et > 0:
                db = db + sc.dbc[axis, p, lines, cols]
            sc.dbc[axis, p, lines, cols] = db
            dw = dw + g * sc.bc[axis, p, lines, cols]
            dr = dr + (g * sc.ah[axis, et, lh, t, n]) * rates[n]
            out.append(a * g)
        sc.ddt[axis, p, lines, lanes] = dr * LN2 + dw * sc.u[axis, p, lines, lanes]
        du = dw * dt + skip * ct
        if axis == 0:
            sc.turned[1, et, pl.ds(pl.multiple_of(p * TS + line0, 8), 8), :] = du
        else:
            sc.field[1, et, p, lines, :] = sc.field[1, et, p, lines, :] + du
        return out

    lax.fori_loop(0, TS, backward, [sc.vals[axis, 1, et, pl.ds(pl.multiple_of(n * TS + line0, 8), 8), :] for n in range(NS)])


def project_back(axis, lines, count, io, sc):
    rows = TS * count
    dt = sc.dt[axis, :, lines, :].reshape(rows, E)
    small = dt * (1.0 - dt * (0.5 - dt * (1.0 / 6.0 - dt * (1.0 / 24.0))))
    dv = sc.ddt[axis, :, lines, :].reshape(rows, E) * jnp.where(dt < 0.03, small, 1.0 - jnp.exp(-dt))
    proj = sc.dw[axis]
    dmix = sum(dot(part, proj, NT) for part in halves(dv))
    row = lax.broadcasted_iota(jnp.int32, (512, 128), 0)
    col = lax.broadcasted_iota(jnp.int32, (512, 128), 1)
    for blk in range(8):
        pick = (col == 12 + blk * 4 + row // 128).astype(jnp.bfloat16)
        for part in halves(sc.dbc[axis, :, lines, blk * 512 : (blk + 1) * 512].reshape(rows, 512)):
            dmix = dmix + dot(part, pick)
    parts = halves(dmix)
    weight = sc.xw[axis]
    xb = sc.u[axis, :, lines, :].reshape(rows, E).astype(jnp.bfloat16)
    return sum(dot(part, xb, TN) for part in parts), sum(dot(part, weight) for part in parts)


class Refs:
    def __init__(self, names, refs):
        self.__dict__.update(zip(names, refs))


INPUTS = ("x", "cot", "xw", "dw", "bias", "alog", "skip")


def layer_kernel(*refs):
    hbm = refs[:7]
    yo_ref, duo_ref, dxo_ref = refs[7:10]
    sc = Refs(SCRATCH, refs[10:])
    io = Refs(INPUTS, [getattr(sc, "in_" + name) for name in INPUTS])
    tile = lax.axis_index("tile")
    side = lax.axis_index("dir")
    other = 1 - side
    row, col = tile // 8, tile % 8
    along_row = [row * 8 + lax.rem(col + d, 8) for d in range(1, 8)]
    along_col = [lax.rem(row + d, 8) * 8 + col for d in range(1, 8)]
    peers = (along_row, along_col)
    depth, plane = tile // 16, tile % 16
    in_plane = [depth * 16 + lax.rem(plane + d, 16) for d in range(1, 16)]
    in_depth = [lax.rem(depth + d, 4) * 16 + plane for d in range(1, 4)]
    beside = (1 - row % 2 + 2 * depth) * 8
    others_near = [beside + lax.rem(col + d, 8) for d in range(1, 8)]
    place = ((col, row), (row, col))
    partner = {"dir": other}

    def turn(i, last):
        return side * last + (1 - 2 * side) * i

    barrier = pltpu.get_barrier_semaphore()
    for peer in along_row + along_col + others_near:
        pl.semaphore_signal(barrier, inc=1, device_id={"tile": peer}, device_id_type=MESH)
    pl.semaphore_signal(barrier, inc=1, device_id=partner, device_id_type=MESH)
    loads = [pltpu.make_async_copy(hbm[k], getattr(sc, "in_" + name), sc.sem_in.at[k]) for k, name in enumerate(INPUTS)]
    for load in loads:
        load.start()
    for load in loads:
        load.wait()

    def push(src, dst, sems, slot, where):
        copy = pltpu.make_async_remote_copy(
            src_ref=src, dst_ref=dst, send_sem=sems.at[(0,) + slot], recv_sem=sems.at[(1,) + slot],
            device_id=where, device_id_type=MESH)
        copy.start()
        return copy

    bands, backs = [[], []], [[], []]

    def map_copy(axis, share, sender, where):
        return pltpu.make_async_remote_copy(
            src_ref=sc.msg.at[axis, share], dst_ref=sc.recv.at[axis, turn(sender, 7)],
            send_sem=sc.sem_there.at[0, axis, share], recv_sem=sc.sem_there.at[1, axis, sender],
            device_id=where, device_id_type=MESH)

    def send_maps(axis):
        pos = place[axis][0]
        sc.recv[axis, turn(pos, 7)] = sc.msg[axis, pos]
        for d in range(1, 8):
            map_copy(axis, lax.rem(pos + d, 8), pos, {"tile": peers[axis][d - 1]}).start()

    def wait_maps(axis, sent):
        pos = place[axis][0]
        for d in range(1, 8):
            peer = lax.rem(pos + d, 8)
            copy = map_copy(axis, peer if sent else 0, pos if sent else peer, {"tile": peers[axis][d - 1]})
            if sent:
                copy.wait_send()
            else:
                copy.wait_recv()

    def fold_and_send(axis):
        pos, band = place[axis]
        wait_maps(axis, False)
        for tau in range(8):
            for et in range(3):
                sc.own_f32[axis, et, tau * TS : (tau + 1) * TS, :] = sc.recv[axis, tau, 4, :, lane_block(et)].astype(jnp.float32)
        fold_lines(axis, pos, turn, sc)
        slot = turn(band, 7)
        bands[axis] = [
            push(sc.band_send.at[axis], sc.band_recv.at[axis, slot], sc.sem_band, (axis, d - 1), {"tile": peers[1 - axis][d - 1]})
            for d in range(1, 8)]
        sc.band_recv[axis, slot] = sc.band_send[axis]

    def enter_and_send(axis):
        pos, band = place[axis]
        for copy in bands[axis]:
            copy.wait_recv()
        enter_lines(axis, pos, turn(band, 7), turn, sc)
        backs[axis] = [
            push(sc.out.at[axis, turn(lax.rem(pos + d, 8), 7)], sc.back.at[axis, pos], sc.sem_back, (axis, d - 1), {"tile": peers[axis][d - 1]})
            for d in range(1, 8)]
        sc.back[axis, pos] = sc.out[axis, turn(pos, 7)]

    prepare(0, io, sc)
    local_maps(0, 0, turn, sc)
    pl.semaphore_wait(barrier, 22)
    local_maps(0, 1, turn, sc)
    send_maps(0)
    prepare(1, io, sc)
    local_maps(1, 0, turn, sc)
    local_maps(1, 1, turn, sc)
    fold_and_send(0)
    send_maps(1)
    enter_and_send(0)
    fold_and_send(1)
    enter_and_send(1)

    halves_sent = [[], []]
    own = pl.ds(pl.multiple_of(side * 8, 8), 8)
    others = pl.ds(pl.multiple_of(other * 8, 8), 8)

    def send_half(kind):
        for et in range(3):
            halves_sent[kind].append(push(sc.field.at[kind, et, :, others, :], sc.half.at[kind, et], sc.sem_half, (kind, et), partner))

    def dx_put(axis, dx):
        for j in range(16):
            sc.dx_src[j, 4 * axis : 4 * axis + 4] = dx[3 * j : 3 * j + 4]

    def dx_first():
        sc.dx_one[plane] = sc.dx_src[plane]
        return [push(sc.dx_src.at[lax.rem(plane + d, 16)], sc.dx_one.at[plane], sc.sem_dx, (0, d - 1), {"tile": in_plane[d - 1]})
                for d in range(1, 16)]

    def dx_next(arriving, phase):
        for copy in arriving:
            copy.wait_recv()
        if phase == 1:
            sc.dx_two[depth] = sum(sc.dx_one[j] for j in range(16))
            part, there = sc.dx_two.at[depth], in_depth
        else:
            sc.dx_all[plane] = sum(sc.dx_two[j] for j in range(4))
            part, there = sc.dx_all.at[plane], in_plane
        return [push(part, part, sc.sem_dx, (phase, k), {"tile": tile_to}) for k, tile_to in enumerate(there)]

    outs = []

    def merge(kind):
        for et in range(3):
            halves_sent[kind][et].wait_recv()
            total = sc.field[kind, et, :, own, :] + sc.half[kind, et]
            sc.res[kind, et, side] = total.reshape(128, 128).astype(jnp.bfloat16)
            outs.append(push(sc.res.at[kind, et, side], sc.res.at[kind, et, side], sc.sem_out, (kind, et), partner))

    def write_out(kind, ref):
        for et in range(3):
            outs[3 * kind + et].wait_recv()
            parts = [sc.res[kind, et, h].astype(jnp.float32).reshape(TS, 8, 128) for h in range(2)]
            ref[:, lane_block(et)] = jnp.concatenate(parts, axis=1).reshape(TOK, 128).astype(jnp.bfloat16)

    def both(fn, axis):
        def unit(lh, carry):
            for et in range(3):
                fn(axis, et, lh, turn, io, sc)
            return carry

        lax.fori_loop(0, 2, unit, 0)

    def to_field(kind):
        for et in range(3):
            for i in range(TS):
                sc.field[kind, et, i] = sc.turned[kind, et, pl.ds(i, TS, stride=TS), :]

    for copy in backs[0]:
        copy.wait_recv()
    decode(0, turn(col, 7), turn, sc)
    both(scan_forward, 0)
    to_field(0)
    for copy in backs[1]:
        copy.wait_recv()
    decode(1, turn(row, 7), turn, sc)
    for et in range(3):
        scan_forward(1, et, other, turn, io, sc)
    send_half(0)
    both(scan_backward, 0)
    dx, through = project_back(0, slice(0, TS), TS, io, sc)
    dx_put(0, dx)
    for et in range(3):
        sc.turned[1, et] = sc.turned[1, et] + through[:, lane_block(et)]
    to_field(1)
    dxs = []
    for lh, lines in ((other, others), (side, own)):
        if lh is side:
            for et in range(3):
                scan_forward(1, et, side, turn, io, sc)
            merge(0)
        for et in range(3):
            scan_backward(1, et, lh, turn, io, sc)
        dx, through = project_back(1, lines, 8, io, sc)
        dxs.append(dx)
        for et in range(3):
            sc.field[1, et, :, lines, :] = sc.field[1, et, :, lines, :] + through[:, lane_block(et)].reshape(TS, 8, 128)
        if lh is other:
            send_half(1)
    dx_put(1, dxs[0] + dxs[1])
    dx_sent = [dx_first()]
    dx_sent.append(dx_next(dx_sent[0], 1))
    merge(1)
    dx_sent.append(dx_next(dx_sent[1], 2))
    write_out(0, yo_ref)
    for copy in dx_sent[2]:
        copy.wait_recv()
    for j in range(15):
        for axis in range(2):
            count = min(3, 44 - 3 * j)
            dxo_ref[3 * j : 3 * j + count, axis, :] = sc.dx_all[j, 4 * axis : 4 * axis + count, :]
    write_out(1, duo_ref)
    for axis in range(2):
        wait_maps(axis, True)
    for group in bands + backs + halves_sent + [outs] + dx_sent:
        for copy in group:
            copy.wait_send()


def f32_buf(*shape):
    return pltpu.VMEM(shape, jnp.float32)


def bf16_buf(*shape):
    return pltpu.VMEM(shape, jnp.bfloat16)


def dma_sems(*shape):
    return pltpu.SemaphoreType.DMA(shape)


BUFFERS = {
    "in_x": bf16_buf(TOK, E), "in_cot": bf16_buf(TOK, E), "in_xw": bf16_buf(44, 2, E), "in_dw": bf16_buf(12, 2, E), "padded": f32_buf(128, E), "xw": bf16_buf(2, 128, E), "dw": bf16_buf(2, 128, E),
    "in_bias": f32_buf(2, E), "in_alog": f32_buf(2, NS, E), "in_skip": f32_buf(2, E), "sem_in": dma_sems(7),
    "u": f32_buf(2, TS, TS, E), "cot": f32_buf(2, TS, TS, E), "dt": f32_buf(2, TS, TS, E), "w": f32_buf(2, TS, TS, E),
    "bc": f32_buf(2, TS, TS, 4096), "rate": f32_buf(2, NS, E), "size": f32_buf(TS, E),
    "vals": f32_buf(2, 2, 3, NS * TS, 128),
    "msg": bf16_buf(2, 8, 5, TS, E), "recv": bf16_buf(2, 8, 5, TS, E),
    "before": f32_buf(2, 3, 8 * TS, 128), "own_f32": f32_buf(2, 3, 8 * TS, 128), "total": f32_buf(2, TS, E),
    "decay": f32_buf(2, 2, 8, TS, E), "line": f32_buf(2, 6, TS, E),
    "band_send": f32_buf(2, 8, E), "band_recv": f32_buf(2, 8, 8, E),
    "ent": f32_buf(4, 3, 8 * TS, 128),
    "out": bf16_buf(2, 8, 4, TS, E), "back": bf16_buf(2, 8, 4, TS, E),
    "dbc": f32_buf(2, TS, TS, 4096), "ah": f32_buf(2, 3, 2, TS, NS, 8, 128), "ddt": f32_buf(2, TS, TS, E),
    "turned": f32_buf(2, 3, TOK, 128), "field": f32_buf(2, 3, TS, TS, 128),
    "half": f32_buf(2, 3, TS, 8, 128), "res": bf16_buf(2, 3, 2, 128, 128),
    "dx_src": f32_buf(16, 8, E), "dx_one": f32_buf(16, 8, E), "dx_two": f32_buf(4, 8, E), "dx_all": f32_buf(16, 8, E),
    "sem_there": dma_sems(2, 2, 8), "sem_band": dma_sems(2, 2, 7), "sem_back": dma_sems(2, 2, 7),
    "sem_half": dma_sems(2, 2, 3), "sem_out": dma_sems(2, 2, 3), "sem_dx": dma_sems(2, 3, 15),
}
SCRATCH = tuple(BUFFERS)
VMEM = pl.BlockSpec(memory_space=pltpu.VMEM)


def local(tiles, cotangent, xproj_w, dtproj_w, dt_bias, a_log, skip_d):
    xw = xproj_w[0].transpose(2, 0, 1)
    dw = dtproj_w[0].transpose(1, 0, 2)
    out = jax.ShapeDtypeStruct((TOK, E), jnp.bfloat16)
    yo, duo, dxo = pl.pallas_call(
        layer_kernel,
        out_shape=(out, out, jax.ShapeDtypeStruct((44, 2, E), jnp.float32)),
        in_specs=[pl.BlockSpec(memory_space=pl.ANY)] * 7,
        out_specs=(VMEM,) * 3,
        scratch_shapes=list(BUFFERS.values()),
        compiler_params=pltpu.CompilerParams(vmem_limit_bytes=56 * 2**20, collective_id=0, has_side_effects=True),
        name="layer",
    )(tiles.reshape(TOK, E), cotangent.reshape(TOK, E), xw, dw, dt_bias[0], a_log[0], skip_d[0])
    return yo.reshape(tiles.shape), duo.reshape(tiles.shape), dxo.transpose(1, 2, 0)[None]


def solution(mesh):
    by_tile = P(("scene", "tile"), None, None, None)
    by_dir = P("dir", None, None, None)
    return jax.shard_map(
        local,
        mesh=mesh,
        in_specs=(by_tile, by_tile, by_dir, by_dir, P("dir", None, None), by_dir, P("dir", None, None)),
        out_specs=(by_tile, by_tile, P(("scene", "dir"), None, None, None)),
        check_vma=False,
    )
```

time: 121 us -> 115 us (0.950)
  Pallas kernels: 114 us -> 110 us
  local copies, waits for them, and re-layouts: 6.05 us -> 3.3 us
    pallas_call x1, Pallas kernels: 114 us -> 110 us  [local(): pl.pallas_call(layer_kernel, out_shape=(out, out, jax.ShapeDtypeStruct((4...]
    pad x2 -> x0, local copies, waits for them, and re-layouts: 1.42 us -> none  [the longest x1 0.72 us: local(): xw = jnp.pad(xproj_w[0], ((0, 0), (0, 0), (0, 84)))]
    unnamed x11 -> x7, local copies, waits for them, and re-layouts: 3.7 us -> 3.3 us
where the time goes in v1:
time: 115 us; the launch traced here: 114 us
  Pallas kernels  110 us (96%)
  local copies, waits for them, and re-layouts  3.3 us (3%)
    pallas_call x1, Pallas kernels, local(): pl.pallas_call(layer_kernel, out_shape=(out, out, jax.ShapeDtypeStruct((4...  110 us
    unnamed x7, local copies, waits for them, and re-layouts  3.3 us

profile of v1, /device:TPU:1, one launch (start us, length us, event | category | flops | bytes accessed | tf_op | source)
XLA Modules:
  0.0 114.4 jit_solution(10313025013060875450)
XLA Ops:
  0.6 110.4 %layer.1 = (bf16[256,384]{1,0:T(8,128)(2,1)}, bf16[256,384]{1,0:T(8,128)(2,1)}, f32[44,2,384]{2,1,0:T(2,128)}) custom-call(bf16[256,384]{1,0:T(8,128)(2,1)} %bitcast.16, bf16[256,384]{1,0:T(8,128)(2,1)} %bitcast.17, bf16[44,2,384]{2,1,0:T(2,128)(2,1)} %bitcast.21, bf16[12,2,384]{2,1,0:T(2,128)(2,1)} %bitcast.23, f32[2,384]{1,0:T(2,128)} %bitcast.24, ...), custom_call_target="tpu_custom_call" | custom-call | tf_op jit(solution)/shard_map/layer/pallas_call | solution.py:638
  111.1 0.0 copy-start
  111.1 1.7 %copy.13 = bf16[1,16,16,384]{3,2,1,0:T(8,128)(2,1)} copy(bf16[1,16,16,384]{3,2,1,0:T(8,128)(2,1)} %bitcast.19) | data formatting | bytes 393216
  112.7 0.0 copy-done
  112.7 0.0 copy-start.1
  112.7 0.7 copy.14
  113.4 0.3 copy-done.1
  113.7 0.7 copy.15
Async XLA Ops:
  111.1 1.7 %copy-start = (bf16[256,384]{1,0:T(8,128)(2,1)S(1)}, bf16[256,384]{1,0:T(8,128)(2,1)}, u32[]{:S(2)}) copy-start(bf16[256,384]{1,0:T(8,128)(2,1)} %get-tuple-element.7) | copy-start | bytes 589828
  112.7 1.0 copy-start.1

commit v2 on v1

--- a/solution.py
+++ b/solution.py
@@ -72,7 +72,10 @@
     dt = jnp.maximum(raw, 0.0) + jnp.log1p(jnp.exp(-jnp.abs(raw)))
     sc.dt[axis] = dt.reshape(TS, TS, E)
     sc.w[axis] = (dt * xs).reshape(TS, TS, E)
-    sc.rate[axis] = -LOG2E * jnp.exp(io.alog[axis])
+    rate = -LOG2E * jnp.exp(io.alog[axis])
+    sc.rate[axis] = rate
+    for n in range(NS):
+        sc.rate8[axis, n] = jnp.broadcast_to(rate[n : n + 1], (8, E))
     size = dt[0:TS]
     for p in range(1, TS):
         size = size + dt[p * TS : (p + 1) * TS]
@@ -288,77 +291,93 @@
     lax.fori_loop(0, TS, add, [jnp.zeros((1, 128), jnp.float32), jnp.zeros((NS, 128), jnp.float32)] * 6)
 
 
-def scan_forward(axis, et, lh, turn, io, sc):
+def scan_forward(axis, lh, turn, io, sc):
     line0 = pl.multiple_of(lh * 8, 8)
     lines = pl.ds(line0, 8)
-    lanes = lane_block(et)
-    rates = [jnp.broadcast_to(sc.rate[axis, n : n + 1, lanes], (8, 128)) for n in range(NS)]
-    skip = jnp.broadcast_to(io.skip[axis : axis + 1, lanes], (8, 128))
-
-    def forward(t, hs):
-        p = turn(t, 15)
-        dt = sc.dt[axis, p, lines, lanes]
-        w = sc.w[axis, p, lines, lanes]
-        ct = sc.cot[axis, p, lines, lanes]
-        y = skip * sc.u[axis, p, lines, lanes]
-        out = []
-        for n in range(NS):
-            a = jnp.exp2(dt * rates[n])
-            ah = a * hs[n]
-            sc.ah[axis, et, lh, t, n] = ah
-            h = ah + w * sc.bc[axis, p, lines, lane_block(n)]
-            cols = lane_block(NS + n)
-            y = y + h * sc.bc[axis, p, lines, cols]
-            dc = h * ct
-            if et > 0:
-                dc = dc + sc.dbc[axis, p, lines, cols]
-            sc.dbc[axis, p, lines, cols] = dc
-            out.append(h)
-        if axis == 0:
-            sc.turned[0, et, pl.ds(pl.multiple_of(p * TS + line0, 8), 8), :] = y
-        else:
-            sc.field[0, et, p, lines, :] = sc.field[0, et, p, lines, :] + y
-        return out
-
-    lax.fori_loop(0, TS, forward, [sc.vals[axis, 0, et, pl.ds(pl.multiple_of(n * TS + line0, 8), 8), :] for n in range(NS)])
-
-
-def scan_backward(axis, et, lh, turn, io, sc):
+    for half in range(2):
+        ns = range(half * 8, half * 8 + 8)
+
+        def forward(t, hs):
+            p = turn(t, 15)
+            dt, w, ct, y = [], [], [], []
+            for et in range(3):
+                lanes = lane_block(et)
+                dt.append(sc.dt[axis, p, lines, lanes])
+                w.append(sc.w[axis, p, lines, lanes])
+                ct.append(sc.cot[axis, p, lines, lanes])
+                y.append(io.skip[axis : axis + 1, lanes] * sc.u[axis, p, lines, lanes] if half == 0 else jnp.zeros((8, 128), jnp.float32))
+            out = []
+            for m, n in enumerate(ns):
+                b = sc.bc[axis, p, lines, lane_block(n)]
+                c = sc.bc[axis, p, lines, lane_block(NS + n)]
+                dc = jnp.zeros((8, 128), jnp.float32)
+                for et in range(3):
+                    a = jnp.exp2(dt[et] * sc.rate8[axis, n, :, lane_block(et)])
+                    ah = a * hs[3 * m + et]
+                    sc.ah[axis, et, lh, t, n] = ah
+                    h = ah + w[et] * b
+                    y[et] = y[et] + h * c
+                    dc = dc + h * ct[et]
+                    out.append(h)
+                sc.dbc[axis, p, lines, lane_block(NS + n)] = dc
+            for et in range(3):
+                if axis == 0:
+                    rows = pl.ds(pl.multiple_of(p * TS + line0, 8), 8)
+                    sc.turned[0, et, rows, :] = y[et] if half == 0 else sc.turned[0, et, rows, :] + y[et]
+                else:
+                    sc.field[0, et, p, lines, :] = sc.field[0, et, p, lines, :] + y[et]
+            return out
+
+        start = [sc.vals[axis, 0, et, pl.ds(pl.multiple_of(n * TS + line0, 8), 8), :] for n in ns for et in range(3)]
+        lax.fori_loop(0, TS, forward, start)
+
+
+def scan_backward(axis, lh, turn, io, sc):
     line0 = pl.multiple_of(lh * 8, 8)
     lines = pl.ds(line0, 8)
-    lanes = lane_block(et)
-    rates = [jnp.broadcast_to(sc.rate[axis, n : n + 1, lanes], (8, 128)) for n in range(NS)]
-    skip = jnp.broadcast_to(io.skip[axis : axis + 1, lanes], (8, 128))
-
-    def backward(i, gs):
-        t = 15 - i
-        p = turn(t, 15)
-        dt = sc.dt[axis, p, lines, lanes]
-        w = sc.w[axis, p, lines, lanes]
-        ct = sc.cot[axis, p, lines, lanes]
-        dw = jnp.zeros((8, 128), jnp.float32)
-        dr = jnp.zeros((8, 128), jnp.float32)
-        out = []
-        for n in range(NS):
-            a = jnp.exp2(dt * rates[n])
-            g = gs[n] + sc.bc[axis, p, lines, lane_block(NS + n)] * ct
-            cols = lane_block(n)
-            db = g * w
-            if et > 0:
-                db = db + sc.dbc[axis, p, lines, cols]
-            sc.dbc[axis, p, lines, cols] = db
-            dw = dw + g * sc.bc[axis, p, lines, cols]
-            dr = dr + (g * sc.ah[axis, et, lh, t, n]) * rates[n]
-            out.append(a * g)
-        sc.ddt[axis, p, lines, lanes] = dr * LN2 + dw * sc.u[axis, p, lines, lanes]
-        du = dw * dt + skip * ct
-        if axis == 0:
-            sc.turned[1, et, pl.ds(pl.multiple_of(p * TS + line0, 8), 8), :] = du
-        else:
-            sc.field[1, et, p, lines, :] = sc.field[1, et, p, lines, :] + du
-        return out
-
-    lax.fori_loop(0, TS, backward, [sc.vals[axis, 1, et, pl.ds(pl.multiple_of(n * TS + line0, 8), 8), :] for n in range(NS)])
+    for half in range(2):
+        ns = range(half * 8, half * 8 + 8)
+
+        def backward(i, gs):
+            t = 15 - i
+            p = turn(t, 15)
+            dt, w, ct, dw, dr = [], [], [], [], []
+            for et in range(3):
+                lanes = lane_block(et)
+                dt.append(sc.dt[axis, p, lines, lanes])
+                w.append(sc.w[axis, p, lines, lanes])
+                ct.append(sc.cot[axis, p, lines, lanes])
+                dw.append(jnp.zeros((8, 128), jnp.float32))
+                dr.append(jnp.zeros((8, 128), jnp.float32))
+            out = []
+            for m, n in enumerate(ns):
+                b = sc.bc[axis, p, lines, lane_block(n)]
+                c = sc.bc[axis, p, lines, lane_block(NS + n)]
+                db = jnp.zeros((8, 128), jnp.float32)
+                for et in range(3):
+                    rate = sc.rate8[axis, n, :, lane_block(et)]
+                    g = gs[3 * m + et] + c * ct[et]
+                    db = db + g * w[et]
+                    dw[et] = dw[et] + g * b
+                    dr[et] = dr[et] + (g * sc.ah[axis, et, lh, t, n]) * rate
+                    out.append(jnp.exp2(dt[et] * rate) * g)
+                sc.dbc[axis, p, lines, lane_block(n)] = db
+            for et in range(3):
+                lanes = lane_block(et)
+                ddt = dr[et] * LN2 + dw[et] * sc.u[axis, p, lines, lanes]
+                sc.ddt[axis, p, lines, lanes] = ddt if half == 0 else sc.ddt[axis, p, lines, lanes] + ddt
+                du = dw[et] * dt[et]
+                if half == 0:
+                    du = du + io.skip[axis : axis + 1, lanes] * ct[et]
+                if axis == 0:
+                    rows = pl.ds(pl.multiple_of(p * TS + line0, 8), 8)
+                    sc.turned[1, et, rows, :] = du if half == 0 else sc.turned[1, et, rows, :] + du
+                else:
+                    sc.field[1, et, p, lines, :] = sc.field[1, et, p, lines, :] + du
+            return out
+
+        start = [sc.vals[axis, 1, et, pl.ds(pl.multiple_of(n * TS + line0, 8), 8), :] for n in ns for et in range(3)]
+        lax.fori_loop(0, TS, backward, start)
 
 
 def project_back(axis, lines, count, io, sc):
@@ -477,8 +496,8 @@
 
     prepare(0, io, sc)
     local_maps(0, 0, turn, sc)
+    local_maps(0, 1, turn, sc)
     pl.semaphore_wait(barrier, 22)
-    local_maps(0, 1, turn, sc)
     send_maps(0)
     prepare(1, io, sc)
     local_maps(1, 0, turn, sc)
@@ -534,8 +553,7 @@
 
     def both(fn, axis):
         def unit(lh, carry):
-            for et in range(3):
-                fn(axis, et, lh, turn, io, sc)
+            fn(axis, lh, turn, io, sc)
             return carry
 
         lax.fori_loop(0, 2, unit, 0)
@@ -553,8 +571,7 @@
     for copy in backs[1]:
         copy.wait_recv()
     decode(1, turn(row, 7), turn, sc)
-    for et in range(3):
-        scan_forward(1, et, other, turn, io, sc)
+    scan_forward(1, other, turn, io, sc)
     send_half(0)
     both(scan_backward, 0)
     dx, through = project_back(0, slice(0, TS), TS, io, sc)
@@ -565,11 +582,9 @@
     dxs = []
     for lh, lines in ((other, others), (side, own)):
         if lh is side:
-            for et in range(3):
-                scan_forward(1, et, side, turn, io, sc)
+            scan_forward(1, side, turn, io, sc)
             merge(0)
-        for et in range(3):
-            scan_backward(1, et, lh, turn, io, sc)
+        scan_backward(1, lh, turn, io, sc)
         dx, through = project_back(1, lines, 8, io, sc)
         dxs.append(dx)
         for et in range(3):
@@ -612,7 +627,7 @@
     "in_x": bf16_buf(TOK, E), "in_cot": bf16_buf(TOK, E), "in_xw": bf16_buf(44, 2, E), "in_dw": bf16_buf(12, 2, E), "padded": f32_buf(128, E), "xw": bf16_buf(2, 128, E), "dw": bf16_buf(2, 128, E),
     "in_bias": f32_buf(2, E), "in_alog": f32_buf(2, NS, E), "in_skip": f32_buf(2, E), "sem_in": dma_sems(7),
     "u": f32_buf(2, TS, TS, E), "cot": f32_buf(2, TS, TS, E), "dt": f32_buf(2, TS, TS, E), "w": f32_buf(2, TS, TS, E),
-    "bc": f32_buf(2, TS, TS, 4096), "rate": f32_buf(2, NS, E), "size": f32_buf(TS, E),
+    "bc": f32_buf(2, TS, TS, 4096), "rate": f32_buf(2, NS, E), "rate8": f32_buf(2, NS, 8, E), "size": f32_buf(TS, E),
     "vals": f32_buf(2, 2, 3, NS * TS, 128),
     "msg": bf16_buf(2, 8, 5, TS, E), "recv": bf16_buf(2, 8, 5, TS, E),
     "before": f32_buf(2, 3, 8 * TS, 128), "own_f32": f32_buf(2, 3, 8 * TS, 128), "total": f32_buf(2, TS, E),

time: 115 us -> 115 us (level)
  no operation moved by 1% of the time
where the time goes in v2:
time: 115 us; the launch traced here: 114 us
  Pallas kernels  110 us (96%)
  local copies, waits for them, and re-layouts  3.3 us (3%)
    pallas_call x1, Pallas kernels, local(): pl.pallas_call(layer_kernel, out_shape=(out, out, jax.ShapeDtypeStruct((4...  110 us
    unnamed x7, local copies, waits for them, and re-layouts  3.3 us

profile of v2, /device:TPU:1, one launch (start us, length us, event | category | flops | bytes accessed | tf_op | source)
XLA Modules:
  0.0 114.4 jit_solution(12321661059893903824)
XLA Ops:
  0.6 110.5 %layer.1 = (bf16[256,384]{1,0:T(8,128)(2,1)}, bf16[256,384]{1,0:T(8,128)(2,1)}, f32[44,2,384]{2,1,0:T(2,128)}) custom-call(bf16[256,384]{1,0:T(8,128)(2,1)} %bitcast.16, bf16[256,384]{1,0:T(8,128)(2,1)} %bitcast.17, bf16[44,2,384]{2,1,0:T(2,128)(2,1)} %bitcast.21, bf16[12,2,384]{2,1,0:T(2,128)(2,1)} %bitcast.23, f32[2,384]{1,0:T(2,128)} %bitcast.24, ...), custom_call_target="tpu_custom_call" | custom-call | tf_op jit(solution)/shard_map/layer/pallas_call | solution.py:653
  111.1 0.0 copy-start
  111.1 1.7 %copy.13 = bf16[1,16,16,384]{3,2,1,0:T(8,128)(2,1)} copy(bf16[1,16,16,384]{3,2,1,0:T(8,128)(2,1)} %bitcast.19) | data formatting | bytes 393216
  112.8 0.0 copy-done
  112.8 0.0 copy-start.1
  112.8 0.7 copy.14
  113.5 0.3 copy-done.1
  113.8 0.7 copy.15
Async XLA Ops:
  111.1 1.7 %copy-start = (bf16[256,384]{1,0:T(8,128)(2,1)S(1)}, bf16[256,384]{1,0:T(8,128)(2,1)}, u32[]{:S(2)}) copy-start(bf16[256,384]{1,0:T(8,128)(2,1)} %get-tuple-element.7) | copy-start | bytes 589828
  112.8 1.0 copy-start.1
